TPU v7x, 32 devices: a whole 2x2x4 slice. The times are simulated.
32 devices in a mesh: dp: 2 (over y), mp: 16 (over z, x, core).
Axes of the slice: x: 2, y: 2, z: 4, core: 2. Of those that a mesh axis runs over, the one named last changes fastest.
Arguments:
- query: bfloat16 [512, 1024], P('dp', 'mp'), may hold values from -0.75 to 0.75
- kv_cache: bfloat16 [1024, 2048], P('dp', 'mp'), may hold values from -4 to 4, as said below
- out_grad: bfloat16 [512, 1024], P('dp', 'mp'), may hold values from -384 to 384
- source_lengths: int32 [2, 8], P('dp'), may hold values from 1 to 128, 512 in all within a row
- target_lengths: int32 [2, 8], P('dp'), may hold values from 1 to 64, 256 in all within a row
- low_rank: bfloat16 [1024, 32], P(('dp', 'mp')), may hold values from -0.125 to 0.125
- adapter_up_matrix: bfloat16 [32, 1024], replicated, may hold values from -0.1875 to 0.1875
Outputs:
- query_grad: bfloat16 [512, 1024], P('dp', 'mp')
- key_gradient: bfloat16 [1024, 1024], P(('dp', 'mp'))
- value_grad: bfloat16 [1024, 1024], P(('dp', 'mp'))
- low_rank_gradient: float32 [1024, 32], P(('dp', 'mp'))
- adapter_up_gradient: float32 [1024, 32], P(('dp', 'mp'))
Inputs may be any that keep to these rules, and one draw needn't show every extreme that they name: `source_lengths`: each row sums to 512; its largest entry is exactly 128. `target_lengths`: each row sums to 256; its largest entry is exactly 64. `kv_cache`: the key columns lie within -0.75 to 0.75.
All inputs are finite; a program needn't handle non-finite values.
Results may differ from a plain program's by a relative error of at most 0.0053.
Values may be sent and summed in bfloat16 or wider, within the bound.
No kernel may reach another device: no remote copies, remote signals or barrier semaphores. Data moves between devices by JAX's collectives and lax.ppermute only.
A program may use at most 64 MiB of HBM per device.

v0:
```python
import functools

import jax
import jax.numpy as jnp
from jax import lax
from jax.experimental import pallas as pl
from jax.experimental.pallas import tpu as pltpu
from jax.sharding import PartitionSpec as P

HS = 64
LANES = 128
CUT = 8

adapter_factor = 2.0

NT = (((1,), (1,)), ((), ()))
TN = (((0,), (0,)), ((), ()))


def dot(left, right, dims):
    return lax.dot_general(left, right, dims, preferred_element_type=jnp.float32)


def group_order(count):
    quarter = count // 4
    bits = quarter.bit_length() - 1
    assert count == 4 << bits
    turned = [sum(((i >> b) & 1) << (bits - 1 - b) for b in range(bits)) for i in range(quarter)]
    order = []
    for low, high in ((1, 2), (0, 3)):
        for i in range(0, quarter, 2):
            first, second = turned[i], turned[i + 1]
            order += [low * quarter + first, high * quarter + second]
            order += [low * quarter + second, high * quarter + first]
    return [count - 1 - place for place in order]


def source_range(source_ref, target_ref, count):
    position = lax.broadcasted_iota(jnp.int32, (1, count), 1)
    first = jnp.zeros((1, count), jnp.int32)
    last = jnp.zeros((1, count), jnp.int32)
    target_start = jnp.int32(0)
    source_start = jnp.int32(0)
    for i in range(source_ref.shape[1]):
        source_end = source_start + source_ref[0, i]
        inside = position >= target_start
        first = jnp.where(inside, source_start, first)
        last = jnp.where(inside, source_end, last)
        target_start = target_start + target_ref[0, i]
        source_start = source_end
    return first, last


def attention_kernel(
    source_any, target_any, query_any, grad_any, kv_any, low_any, query_grad_ref, sent_ref, turned_ref,
    source_ref, target_ref, query_ref, grad_ref, kv_ref, low_ref, sems,
):
    pairs = [
        (kv_any, kv_ref), (query_any, query_ref), (grad_any, grad_ref),
        (source_any, source_ref), (target_any, target_ref), (low_any, low_ref),
    ]
    copies = [
        pltpu.make_async_copy(here, there, sems.at[i]) for i, (here, there) in enumerate(pairs)
    ]
    for copy in copies:
        copy.start()
    for copy in copies:
        copy.wait()
    tgt_count = query_ref.shape[1]
    both = kv_ref[...]
    query_t = query_ref[...]
    grad_t = grad_ref[...]
    blank = jnp.zeros_like(query_t)
    query_wide = jnp.concatenate([query_t, blank], axis=0)
    grad_wide = jnp.concatenate([blank, grad_t], axis=0)
    scores = jnp.dot(both, query_wide, preferred_element_type=jnp.float32)
    dprob = jnp.dot(both, grad_wide, preferred_element_type=jnp.float32)
    first, last = source_range(source_ref, target_ref, tgt_count)
    position = lax.broadcasted_iota(jnp.int32, scores.shape, 0)
    allowed = jnp.logical_and(position >= first, position < last)
    expo = jnp.where(allowed, jnp.exp(scores), 0.0)
    total = jnp.sum(expo, axis=0, keepdims=True)
    delta = jnp.sum(expo * dprob, axis=0, keepdims=True) / total
    prob = expo * (1.0 / total)
    prob_low = prob.astype(jnp.bfloat16)
    dscore = (prob * (dprob - delta)).astype(jnp.bfloat16)
    both_grad = dot(dscore, query_wide, NT) + dot(prob_low, grad_wide, NT)
    both_low = both_grad.astype(jnp.bfloat16)
    low = low_ref[...].astype(jnp.float32)
    rows = low.shape[0]
    blocks = sent_ref.shape[0]
    packed = jnp.concatenate([low[at:at + CUT] for at in range(0, rows, CUT)], axis=1)
    packed = packed.astype(jnp.bfloat16)
    for at, block in enumerate(group_order(blocks)):
        sent_ref[at, :rows, :] = both_low[block * rows:(block + 1) * rows]
        sent_ref[at, rows:, :] = packed

    wide = both_low.astype(jnp.float32)
    parts = []
    for start in range(0, rows, CUT):
        for block in range(blocks):
            parts.append(wide[block * rows + start:block * rows + start + CUT])
    turned_ref[...] = jnp.concatenate(parts, axis=0).T.astype(jnp.bfloat16)

    query_grad = dot(both, dscore, TN)
    query_grad_ref[...] = query_grad[:HS].astype(jnp.bfloat16)


def split_kernel(turned_ref, *out_refs):
    dp = len(out_refs)
    step = HS // dp
    turned = turned_ref[...].astype(jnp.float32)
    pieces = []
    for j in range(dp):
        rows = [turned[j * step:(j + 1) * step], turned[HS + j * step:HS + (j + 1) * step]]
        pieces.append(jnp.concatenate(rows, axis=0))
    mine = lax.rem(lax.axis_index("mp"), dp)
    for s, out_ref in enumerate(out_refs):
        turn = lax.rem(mine + s, dp)
        chosen = pieces[0]
        for j in range(1, dp):
            chosen = jnp.where(turn == j, pieces[j], chosen)
        out_ref[...] = chosen.astype(jnp.bfloat16)


def order_kernel(*refs):
    *arrived_refs, out_ref = refs
    dp = len(arrived_refs)
    mine = lax.rem(lax.axis_index("mp"), dp)
    for s, arrived_ref in enumerate(arrived_refs):
        out_ref[lax.rem(mine + dp - s, dp)] = arrived_ref[...]


def share_kernel(rows, both_rank, got_ref, pieces_ref, *out_refs):
    dp, piece_rows, _ = pieces_ref.shape
    blocks = got_ref.shape[0]
    order = group_order(blocks)
    lows = [
        got_ref[order.index(block), rows:, :].astype(jnp.float32) for block in range(blocks)
    ]
    lows = jnp.concatenate(lows, axis=0).astype(jnp.bfloat16)
    columns = jnp.concatenate([pieces_ref[e] for e in range(dp)], axis=0)
    share = None
    for cut in range(rows // CUT):
        tokens = columns[:, cut * blocks * CUT:(cut + 1) * blocks * CUT]
        product = jnp.dot(tokens, lows, preferred_element_type=jnp.float32)
        part = product[:, cut * both_rank:(cut + 1) * both_rank]
        share = part if share is None else share + part
    step = piece_rows // 2
    column = lax.broadcasted_iota(jnp.int32, (step, both_rank), 1)
    shares = []
    for e in range(dp):
        keys = share[e * piece_rows:e * piece_rows + step]
        values = share[e * piece_rows + step:(e + 1) * piece_rows]
        shares.append(adapter_factor * jnp.where(column < both_rank // 2, keys, values))
    mine = lax.axis_index("dp")
    for s, out_ref in enumerate(out_refs):
        turn = lax.rem(mine + s, dp)
        chosen = shares[0]
        for e in range(1, dp):
            chosen = jnp.where(turn == e, shares[e], chosen)
        out_ref[...] = chosen


def owner_kernel(got_ref, up_ref, key_ref, value_ref, low_grad_ref):
    rows = key_ref.shape[0]
    rank = up_ref.shape[0] // 2
    order = group_order(got_ref.shape[0])
    for pair in range(len(order) // 2):
        first = got_ref[order.index(2 * pair), :rows, :]
        second = got_ref[order.index(2 * pair + 1), :rows, :]
        columns = slice(2 * pair * HS, (2 * pair + 2) * HS)
        key_ref[:, columns] = jnp.concatenate([first[:, :HS], second[:, :HS]], axis=1)
        value_ref[:, columns] = jnp.concatenate([first[:, HS:], second[:, HS:]], axis=1)
    up = up_ref[...]
    from_key = dot(key_ref[...], up, NT)
    from_value = dot(value_ref[...], up, NT)
    column = lax.broadcasted_iota(jnp.int32, from_key.shape, 1)
    low_grad_ref[...] = adapter_factor * jnp.where(column < rank, from_key, from_value)


def local(dp, mp, query, kv_cache, out_grad, source_lengths, target_lengths, low_rank, adapter_up_matrix):
    tgt_count = query.shape[0]
    src_count = kv_cache.shape[0]
    rows, both_rank = low_rank.shape
    width = adapter_up_matrix.shape[1]
    step = HS // dp
    assert rows // CUT * both_rank == LANES
    vmem = pl.BlockSpec(memory_space=pltpu.VMEM)
    hbm = pl.BlockSpec(memory_space=pl.ANY)
    params = pltpu.CompilerParams(vmem_limit_bytes=48 * 1024 * 1024)
    whole_vmem = pltpu.CompilerParams(vmem_limit_bytes=60 * 1024 * 1024)

    query_t = query.T
    grad_t = out_grad.T
    query_grad_t, sent, turned = pl.pallas_call(
        attention_kernel,
        out_shape=[
            jax.ShapeDtypeStruct((HS, tgt_count), jnp.bfloat16),
            jax.ShapeDtypeStruct((mp, rows + CUT, LANES), jnp.bfloat16),
            jax.ShapeDtypeStruct((2 * HS, src_count), jnp.bfloat16),
        ],
        in_specs=[hbm] * 6,
        out_specs=[vmem] * 3,
        scratch_shapes=[
            pltpu.SMEM(source_lengths.shape, jnp.int32),
            pltpu.SMEM(target_lengths.shape, jnp.int32),
            pltpu.VMEM(query_t.shape, jnp.bfloat16),
            pltpu.VMEM(grad_t.shape, jnp.bfloat16),
            pltpu.VMEM(kv_cache.shape, jnp.bfloat16),
            pltpu.VMEM(low_rank.shape, jnp.bfloat16),
            pltpu.SemaphoreType.DMA((6,)),
        ],
        compiler_params=whole_vmem,
        name="attention_backward",
    )(source_lengths, target_lengths, query_t, grad_t, kv_cache, low_rank)

    route = [(h, h * dp % mp + h * dp // mp) for h in range(mp)]
    pieces = pl.pallas_call(
        split_kernel,
        out_shape=[jax.ShapeDtypeStruct((2 * step, src_count), jnp.bfloat16)] * dp,
        in_specs=[vmem],
        out_specs=[vmem] * dp,
        compiler_params=params,
        cost_estimate=pl.CostEstimate(flops=2 ** 36, bytes_accessed=2 ** 28, transcendentals=0),
        name="split_columns",
    )(lax.ppermute(turned, "mp", route))
    arrived = [pieces[0]]
    for s in range(1, dp):
        route = [(m, m - m % dp + (m + s) % dp) for m in range(mp)]
        arrived.append(lax.ppermute(pieces[s], "mp", route))
    ordered = pl.pallas_call(
        order_kernel,
        out_shape=jax.ShapeDtypeStruct((dp, 2 * step, src_count), jnp.bfloat16),
        in_specs=[vmem] * dp,
        out_specs=vmem,
        compiler_params=params,
        name="order_pieces",
    )(*arrived)

    got = lax.all_to_all(sent, "mp", 0, 0, axis_index_groups=[group_order(mp)], tiled=True)

    shares = pl.pallas_call(
        functools.partial(share_kernel, rows, both_rank),
        out_shape=[jax.ShapeDtypeStruct((step, both_rank), jnp.float32)] * dp,
        in_specs=[vmem] * 2,
        out_specs=[vmem] * dp,
        compiler_params=params,
        name="adapter_shares",
    )(got, ordered)
    up_grad = shares[0]
    for s in range(1, dp):
        route = [(d, (d + s) % dp) for d in range(dp)]
        up_grad = up_grad + lax.ppermute(shares[s], "dp", route)

    key_gradient, value_grad, low_grad = pl.pallas_call(
        owner_kernel,
        out_shape=[
            jax.ShapeDtypeStruct((rows, width), jnp.bfloat16),
            jax.ShapeDtypeStruct((rows, width), jnp.bfloat16),
            jax.ShapeDtypeStruct((rows, both_rank), jnp.float32),
        ],
        in_specs=[vmem] * 2,
        out_specs=[vmem] * 3,
        compiler_params=params,
        name="owner_outputs",
    )(got, adapter_up_matrix)
    return query_grad_t.T, key_gradient, value_grad, low_grad, up_grad


def solution(mesh):
    in_specs = (
        P("dp", "mp"),
        P("dp", "mp"),
        P("dp", "mp"),
        P("dp", None),
        P("dp", None),
        P(("dp", "mp"), None),
        P(),
    )
    out_specs = (
        P("dp", "mp"),
        P(("dp", "mp"), None),
        P(("dp", "mp"), None),
        P(("dp", "mp"), None),
        P(("dp", "mp"), None),
    )
    body = functools.partial(local, mesh.shape["dp"], mesh.shape["mp"])
    return jax.shard_map(body, mesh=mesh, in_specs=in_specs, out_specs=out_specs, check_vma=False)
```

profile of v0, /device:TPU:0, one launch (start us, length us, event | category | flops | bytes accessed | tf_op | source)
XLA Modules:
  0.0 23.9 jit_solution(3443746277614478974)
XLA Ops:
  0.6 2.5 %attention_backward.1 = (bf16[64,256]{1,0:T(8,128)(2,1)}, bf16[16,40,128]{2,1,0:T(8,128)(2,1)}, bf16[128,512]{1,0:T(8,128)(2,1)}) custom-call(s32[1,8]{1,0:T(1,128)} %source_any.1, s32[1,8]{1,0:T(1,128)} %target_any.1, bf16[64,256]{1,0:T(8,128)(2,1)} %bitcast.3, bf16[64,256]{1,0:T(8,128)(2,1)} %bitcast.4, bf16[512,128]{1,0:T(8,128)(2,1)} %kv_any.1, ...), custom_call_target="tpu_custom_call" | custom-call | tf_op jit(solution)/shard_map/attention_backward/pallas_call | solution.py:196
  3.1 1.6 %collective-permute-start = (bf16[128,512]{1,0:T(8,128)(2,1)}, bf16[128,512]{1,0:T(8,128)(2,1)S(1)}, u32[]{:S(2)}, u32[]{:S(2)}) collective-permute-start(bf16[128,512]{1,0:T(8,128)(2,1)} %get-tuple-element.20), channel_id=1, source_target_pairs={{0,0},{1,2},{2,4},{3,6},{4,8},{5,10},{6,12},{7,14},{8,1},{9,3},{10... | collective-permute-start | bytes 393224 | tf_op jit(solution)/shard_map/ppermute | solution.py:227
  4.7 9.4 %all-to-all-start = ((bf16[16,40,128]{2,1,0:T(8,128)(2,1)}), bf16[16,40,128]{2,1,0:T(8,128)(2,1)S(1)}, u32[]{:S(2)}, u32[]{:S(2)}) async-start(bf16[16,40,128]{2,1,0:T(8,128)(2,1)} %get-tuple-element.16), calls=%async_computation | async-start | bytes 327680 | tf_op jit(solution)/shard_map/all_to_all | solution.py:241
  14.1 0.0 collective-permute-done.turned_ref
  14.1 0.1 collective-permute-start.1
  14.3 1.2 %collective-permute-done.1.refs_1_ = bf16[64,512]{1,0:T(8,128)(2,1)S(1)} collective-permute-done((bf16[64,512]{1,0:T(8,128)(2,1)S(1)}, bf16[64,512]{1,0:T(8,128)(2,1)S(1)}, u32[]{:S(2)}, u32[]{:S(2)}) %collective-permute-start.1) | collective-permute-done | bytes 65568 | tf_op jit(solution)/shard_map/ppermute | solution.py:231
  15.5 0.0 copy-start
  15.5 3.8 %all-to-all-done.got_ref = bf16[16,40,128]{2,1,0:T(8,128)(2,1)S(1)} async-done(((bf16[16,40,128]{2,1,0:T(8,128)(2,1)}), bf16[16,40,128]{2,1,0:T(8,128)(2,1)S(1)}, u32[]{:S(2)}, u32[]{:S(2)}) %all-to-all-start) | async-done | bytes 163872 | tf_op jit(solution)/shard_map/all_to_all | solution.py:241
  19.2 0.3 %adapter_shares.1 = (f32[32,32]{1,0:T(8,128)S(1)}, f32[32,32]{1,0:T(8,128)S(1)}) custom-call(bf16[16,40,128]{2,1,0:T(8,128)(2,1)S(1)} %all-to-all-done.got_ref, bf16[2,64,512]{2,1,0:T(8,128)(2,1)S(1)} %order_pieces.1.pieces_ref), custom_call_target="tpu_custom_call" | custom-call | tf_op jit(solution)/shard_map/adapter_shares/pallas_call | solution.py:243
  19.5 1.6 %collective-permute-start.2 = (f32[32,32]{1,0:T(8,128)S(1)}, f32[32,32]{1,0:T(8,128)S(1)}, u32[]{:S(2)}, u32[]{:S(2)}) collective-permute-start(f32[32,32]{1,0:T(8,128)S(1)} %get-tuple-element.24), channel_id=1, source_target_pairs={{0,16},{16,0},{1,17},{17,1},{2,18},{18,2},{3,19},{19,3},{4,20},{20... | collective-permute-start | bytes 12296 | tf_op jit(solution)/shard_map/ppermute | solution.py:254
  21.1 0.0 copy-done
  21.1 0.9 %owner_outputs.1 = (bf16[32,1024]{1,0:T(8,128)(2,1)}, bf16[32,1024]{1,0:T(8,128)(2,1)}, f32[32,32]{1,0:T(8,128)}) custom-call(bf16[16,40,128]{2,1,0:T(8,128)(2,1)S(1)} %all-to-all-done.got_ref, bf16[32,1024]{1,0:T(8,128)(2,1)S(1)} %copy-done), custom_call_target="tpu_custom_call" | custom-call | tf_op jit(solution)/shard_map/owner_outputs/pallas_call | solution.py:256
  22.0 1.4 %collective-permute-done.2 = f32[32,32]{1,0:T(8,128)S(1)} collective-permute-done((f32[32,32]{1,0:T(8,128)S(1)}, f32[32,32]{1,0:T(8,128)S(1)}, u32[]{:S(2)}, u32[]{:S(2)}) %collective-permute-start.2) | collective-permute-done | bytes 4128 | tf_op jit(solution)/shard_map/ppermute | solution.py:254
  23.3 0.6 %add.3 = f32[32,32]{1,0:T(8,128)} add(f32[32,32]{1,0:T(8,128)S(1)} %get-tuple-element.23, f32[32,32]{1,0:T(8,128)S(1)} %collective-permute-done.2) | non-fusion elementwise | flops 1024 | bytes 12288 | tf_op jit(solution)/shard_map/add | solution.py:254
  (2 shorter events, 0.1 us)
Async XLA Ops:
  3.1 11.0 %collective-permute-start = (bf16[128,512]{1,0:T(8,128)(2,1)}, bf16[128,512]{1,0:T(8,128)(2,1)S(1)}, u32[]{:S(2)}, u32[]{:S(2)}) collective-permute-start(bf16[128,512]{1,0:T(8,128)(2,1)} %get-tuple-element.20), channel_id=1, source_target_pairs={{0,0},{1,2},{2,4},{3,6},{4,8},{5,10},{6,12},{7,14},{8,1},{9,3},{10... | collective-permute-start | bytes 393224 | tf_op jit(solution)/shard_map/ppermute | solution.py:227
  4.7 14.6 %all-to-all-start = ((bf16[16,40,128]{2,1,0:T(8,128)(2,1)}), bf16[16,40,128]{2,1,0:T(8,128)(2,1)S(1)}, u32[]{:S(2)}, u32[]{:S(2)}) async-start(bf16[16,40,128]{2,1,0:T(8,128)(2,1)} %get-tuple-element.16), calls=%async_computation | async-start | bytes 327680 | tf_op jit(solution)/shard_map/all_to_all | solution.py:241
  14.1 1.3 %collective-permute-start.1 = (bf16[64,512]{1,0:T(8,128)(2,1)S(1)}, bf16[64,512]{1,0:T(8,128)(2,1)S(1)}, u32[]{:S(2)}, u32[]{:S(2)}) collective-permute-start(bf16[64,512]{1,0:T(8,128)(2,1)S(1)} %get-tuple-element.22), channel_id=1, source_target_pairs={{0,1},{1,0},{2,3},{3,2},{4,5},{5,4},{6,7},{7,6},{8,9},{9,8},{10,11... | collective-permute-start | bytes 196616 | tf_op jit(solution)/shard_map/ppermute | solution.py:231
  15.5 5.6 %copy-start = (bf16[32,1024]{1,0:T(8,128)(2,1)S(1)}, bf16[32,1024]{1,0:T(8,128)(2,1)}, u32[]{:S(2)}) copy-start(bf16[32,1024]{1,0:T(8,128)(2,1)} %up_ref.1) | copy-start | bytes 196612
  19.5 3.8 %collective-permute-start.2 = (f32[32,32]{1,0:T(8,128)S(1)}, f32[32,32]{1,0:T(8,128)S(1)}, u32[]{:S(2)}, u32[]{:S(2)}) collective-permute-start(f32[32,32]{1,0:T(8,128)S(1)} %get-tuple-element.24), channel_id=1, source_target_pairs={{0,16},{16,0},{1,17},{17,1},{2,18},{18,2},{3,19},{19,3},{4,20},{20... | collective-permute-start | bytes 12296 | tf_op jit(solution)/shard_map/ppermute | solution.py:254
where the time goes:
time: 24.2 us; the launch traced here: 23.9 us
  starting transfers between devices  12.7 us (52%)
  waiting for transfers between devices  6.31 us (26%)
  Pallas kernels  3.65 us (15%)
  between operations  0.68 us (3%)
  other arithmetic  0.61 us (3%)
    all_to_all x1, starting transfers between devices, local(): lax.all_to_all(sent, 'mp', 0, 0, axis_index_groups=[group_order(mp)], til...  9.39 us
    all_to_all x1, waiting for transfers between devices, local(): lax.all_to_all(sent, 'mp', 0, 0, axis_index_groups=[group_order(mp)], til...  3.77 us
    pallas_call x1, Pallas kernels, local(): pl.pallas_call(attention_kernel, out_shape=[jax.ShapeDtypeStruct((HS, tgt...  2.48 us
    ppermute x1, starting transfers between devices, local(): up_grad = up_grad + lax.ppermute(shares[s], 'dp', route)  1.58 us
    ppermute x1, starting transfers between devices, local(): lax.ppermute(turned, 'mp', route)  1.56 us
    ppermute x1, waiting for transfers between devices, local(): up_grad = up_grad + lax.ppermute(shares[s], 'dp', route)  1.36 us
    ppermute x1, waiting for transfers between devices, local(): arrived.append(lax.ppermute(pieces[s], 'mp', route))  1.17 us
    pallas_call x1, Pallas kernels, local(): pl.pallas_call(owner_kernel, out_shape=[jax.ShapeDtypeStruct((rows, width...  0.86 us
  transfers between devices with their start and end apart: 4, of which 3 were waited for; matrix products, arithmetic and copies ran while one was open for 0% of the time, Pallas kernels for 4%

commit v1 on v0

--- a/solution.py
+++ b/solution.py
@@ -114,9 +114,10 @@
     for j in range(dp):
         rows = [turned[j * step:(j + 1) * step], turned[HS + j * step:HS + (j + 1) * step]]
         pieces.append(jnp.concatenate(rows, axis=0))
-    mine = lax.rem(lax.axis_index("mp"), dp)
+    e = lax.rem(lax.axis_index("mp"), dp)
+    pack = lax.axis_index("dp")
     for s, out_ref in enumerate(out_refs):
-        turn = lax.rem(mine + s, dp)
+        turn = lax.rem(2 * e + s + dp - pack, dp)
         chosen = pieces[0]
         for j in range(1, dp):
             chosen = jnp.where(turn == j, pieces[j], chosen)
@@ -250,8 +251,11 @@
     )(got, ordered)
     up_grad = shares[0]
     for s in range(1, dp):
-        route = [(d, (d + s) % dp) for d in range(dp)]
-        up_grad = up_grad + lax.ppermute(shares[s], "dp", route)
+        route = [
+            (d * mp + m, (d + s) % dp * mp + m - m % dp + (m + s) % dp)
+            for d in range(dp) for m in range(mp)
+        ]
+        up_grad = up_grad + lax.ppermute(shares[s], ("dp", "mp"), route)
 
     key_gradient, value_grad, low_grad = pl.pallas_call(
         owner_kernel,

time: 24.2 us -> 23.7 us (0.979)
  starting transfers between devices: 12.7 us -> 12 us
    ppermute x1, starting transfers between devices: 1.58 us -> 0.95 us  [local(): up_grad = up_grad + lax.ppermute(shares[s], ('dp', 'mp'), route)]
where the time goes in v1:
time: 23.7 us; the launch traced here: 23.4 us
  starting transfers between devices  12 us (51%)
  waiting for transfers between devices  6.46 us (27%)
  Pallas kernels  3.65 us (15%)
  between operations  0.68 us (3%)
  other arithmetic  0.61 us (3%)
    all_to_all x1, starting transfers between devices, local(): lax.all_to_all(sent, 'mp', 0, 0, axis_index_groups=[group_order(mp)], til...  9.39 us
    all_to_all x1, waiting for transfers between devices, local(): lax.all_to_all(sent, 'mp', 0, 0, axis_index_groups=[group_order(mp)], til...  3.77 us
    pallas_call x1, Pallas kernels, local(): pl.pallas_call(attention_kernel, out_shape=[jax.ShapeDtypeStruct((HS, tgt...  2.48 us
    ppermute x1, starting transfers between devices, local(): lax.ppermute(turned, 'mp', route)  1.56 us
    ppermute x1, waiting for transfers between devices, local(): up_grad = up_grad + lax.ppermute(shares[s], ('dp', 'mp'), route)  1.52 us
    ppermute x1, waiting for transfers between devices, local(): arrived.append(lax.ppermute(pieces[s], 'mp', route))  1.17 us
    ppermute x1, starting transfers between devices, local(): up_grad = up_grad + lax.ppermute(shares[s], ('dp', 'mp'), route)  0.95 us
    pallas_call x1, Pallas kernels, local(): pl.pallas_call(owner_kernel, out_shape=[jax.ShapeDtypeStruct((rows, width...  0.86 us
  transfers between devices with their start and end apart: 4, of which 3 were waited for; matrix products, arithmetic and copies ran while one was open for 0% of the time, Pallas kernels for 4%

profile of v1, /device:TPU:0, one launch (start us, length us, event | category | flops | bytes accessed | tf_op | source)
XLA Modules:
  0.0 23.4 jit_solution(3229956081721014859)
XLA Ops:
  0.6 2.5 %attention_backward.1 = (bf16[64,256]{1,0:T(8,128)(2,1)}, bf16[16,40,128]{2,1,0:T(8,128)(2,1)}, bf16[128,512]{1,0:T(8,128)(2,1)}) custom-call(s32[1,8]{1,0:T(1,128)} %source_any.1, s32[1,8]{1,0:T(1,128)} %target_any.1, bf16[64,256]{1,0:T(8,128)(2,1)} %bitcast.3, bf16[64,256]{1,0:T(8,128)(2,1)} %bitcast.4, bf16[512,128]{1,0:T(8,128)(2,1)} %kv_any.1, ...), custom_call_target="tpu_custom_call" | custom-call | tf_op jit(solution)/shard_map/attention_backward/pallas_call | solution.py:197
  3.1 1.6 %collective-permute-start = (bf16[128,512]{1,0:T(8,128)(2,1)}, bf16[128,512]{1,0:T(8,128)(2,1)S(1)}, u32[]{:S(2)}, u32[]{:S(2)}) collective-permute-start(bf16[128,512]{1,0:T(8,128)(2,1)} %get-tuple-element.20), channel_id=1, source_target_pairs={{0,0},{1,2},{2,4},{3,6},{4,8},{5,10},{6,12},{7,14},{8,1},{9,3},{10... | collective-permute-start | bytes 393224 | tf_op jit(solution)/shard_map/ppermute | solution.py:228
  4.7 9.4 %all-to-all-start = ((bf16[16,40,128]{2,1,0:T(8,128)(2,1)}), bf16[16,40,128]{2,1,0:T(8,128)(2,1)S(1)}, u32[]{:S(2)}, u32[]{:S(2)}) async-start(bf16[16,40,128]{2,1,0:T(8,128)(2,1)} %get-tuple-element.16), calls=%async_computation | async-start | bytes 327680 | tf_op jit(solution)/shard_map/all_to_all | solution.py:242
  14.1 0.0 collective-permute-done.turned_ref
  14.1 0.1 collective-permute-start.1
  14.3 1.2 %collective-permute-done.1.refs_1_ = bf16[64,512]{1,0:T(8,128)(2,1)S(1)} collective-permute-done((bf16[64,512]{1,0:T(8,128)(2,1)S(1)}, bf16[64,512]{1,0:T(8,128)(2,1)S(1)}, u32[]{:S(2)}, u32[]{:S(2)}) %collective-permute-start.1) | collective-permute-done | bytes 65568 | tf_op jit(solution)/shard_map/ppermute | solution.py:232
  15.5 0.0 copy-start
  15.5 3.8 %all-to-all-done.got_ref = bf16[16,40,128]{2,1,0:T(8,128)(2,1)S(1)} async-done(((bf16[16,40,128]{2,1,0:T(8,128)(2,1)}), bf16[16,40,128]{2,1,0:T(8,128)(2,1)S(1)}, u32[]{:S(2)}, u32[]{:S(2)}) %all-to-all-start) | async-done | bytes 163872 | tf_op jit(solution)/shard_map/all_to_all | solution.py:242
  19.2 0.3 %adapter_shares.1 = (f32[32,32]{1,0:T(8,128)S(1)}, f32[32,32]{1,0:T(8,128)S(1)}) custom-call(bf16[16,40,128]{2,1,0:T(8,128)(2,1)S(1)} %all-to-all-done.got_ref, bf16[2,64,512]{2,1,0:T(8,128)(2,1)S(1)} %order_pieces.1.pieces_ref), custom_call_target="tpu_custom_call" | custom-call | tf_op jit(solution)/shard_map/adapter_shares/pallas_call | solution.py:244
  19.5 0.9 %collective-permute-start.2 = (f32[32,32]{1,0:T(8,128)S(1)}, f32[32,32]{1,0:T(8,128)S(1)}, u32[]{:S(2)}, u32[]{:S(2)}) collective-permute-start(f32[32,32]{1,0:T(8,128)S(1)} %get-tuple-element.24), channel_id=1, source_target_pairs={{0,17},{1,16},{2,19},{3,18},{4,21},{5,20},{6,23},{7,22},{8,25},{9,... | collective-permute-start | bytes 12296 | tf_op jit(solution)/shard_map/ppermute | solution.py:258
  20.5 0.0 copy-done
  20.5 0.9 %owner_outputs.1 = (bf16[32,1024]{1,0:T(8,128)(2,1)}, bf16[32,1024]{1,0:T(8,128)(2,1)}, f32[32,32]{1,0:T(8,128)}) custom-call(bf16[16,40,128]{2,1,0:T(8,128)(2,1)S(1)} %all-to-all-done.got_ref, bf16[32,1024]{1,0:T(8,128)(2,1)S(1)} %copy-done), custom_call_target="tpu_custom_call" | custom-call | tf_op jit(solution)/shard_map/owner_outputs/pallas_call | solution.py:260
  21.3 1.5 %collective-permute-done.2 = f32[32,32]{1,0:T(8,128)S(1)} collective-permute-done((f32[32,32]{1,0:T(8,128)S(1)}, f32[32,32]{1,0:T(8,128)S(1)}, u32[]{:S(2)}, u32[]{:S(2)}) %collective-permute-start.2) | collective-permute-done | bytes 4128 | tf_op jit(solution)/shard_map/ppermute | solution.py:258
  22.8 0.6 %add.3 = f32[32,32]{1,0:T(8,128)} add(f32[32,32]{1,0:T(8,128)S(1)} %get-tuple-element.23, f32[32,32]{1,0:T(8,128)S(1)} %collective-permute-done.2) | non-fusion elementwise | flops 1024 | bytes 12288 | tf_op jit(solution)/shard_map/add | solution.py:258
  (2 shorter events, 0.1 us)
Async XLA Ops:
  3.1 11.0 %collective-permute-start = (bf16[128,512]{1,0:T(8,128)(2,1)}, bf16[128,512]{1,0:T(8,128)(2,1)S(1)}, u32[]{:S(2)}, u32[]{:S(2)}) collective-permute-start(bf16[128,512]{1,0:T(8,128)(2,1)} %get-tuple-element.20), channel_id=1, source_target_pairs={{0,0},{1,2},{2,4},{3,6},{4,8},{5,10},{6,12},{7,14},{8,1},{9,3},{10... | collective-permute-start | bytes 393224 | tf_op jit(solution)/shard_map/ppermute | solution.py:228
  4.7 14.6 %all-to-all-start = ((bf16[16,40,128]{2,1,0:T(8,128)(2,1)}), bf16[16,40,128]{2,1,0:T(8,128)(2,1)S(1)}, u32[]{:S(2)}, u32[]{:S(2)}) async-start(bf16[16,40,128]{2,1,0:T(8,128)(2,1)} %get-tuple-element.16), calls=%async_computation | async-start | bytes 327680 | tf_op jit(solution)/shard_map/all_to_all | solution.py:242
  14.1 1.3 %collective-permute-start.1 = (bf16[64,512]{1,0:T(8,128)(2,1)S(1)}, bf16[64,512]{1,0:T(8,128)(2,1)S(1)}, u32[]{:S(2)}, u32[]{:S(2)}) collective-permute-start(bf16[64,512]{1,0:T(8,128)(2,1)S(1)} %get-tuple-element.22), channel_id=1, source_target_pairs={{0,1},{1,0},{2,3},{3,2},{4,5},{5,4},{6,7},{7,6},{8,9},{9,8},{10,11... | collective-permute-start | bytes 196616 | tf_op jit(solution)/shard_map/ppermute | solution.py:232
  15.5 5.0 %copy-start = (bf16[32,1024]{1,0:T(8,128)(2,1)S(1)}, bf16[32,1024]{1,0:T(8,128)(2,1)}, u32[]{:S(2)}) copy-start(bf16[32,1024]{1,0:T(8,128)(2,1)} %up_ref.1) | copy-start | bytes 196612
  19.5 3.3 %collective-permute-start.2 = (f32[32,32]{1,0:T(8,128)S(1)}, f32[32,32]{1,0:T(8,128)S(1)}, u32[]{:S(2)}, u32[]{:S(2)}) collective-permute-start(f32[32,32]{1,0:T(8,128)S(1)} %get-tuple-element.24), channel_id=1, source_target_pairs={{0,17},{1,16},{2,19},{3,18},{4,21},{5,20},{6,23},{7,22},{8,25},{9,... | collective-permute-start | bytes 12296 | tf_op jit(solution)/shard_map/ppermute | solution.py:258
